TPU v7x, 512 devices: a whole 4x8x8 slice. The times are simulated.
512 devices in a mesh: expert: 64 (over y, z), tensor: 8 (over x, core).
Axes of the slice: x: 4, y: 8, z: 8, core: 2. Of those that a mesh axis runs over, the one named last changes fastest.
Arguments:
- patches: bfloat16 [32768, 1664], P('expert', 'tensor'), may hold values from -6 to 6
- expert_ids: int32 [32768, 2], P('expert'), may hold values from 0 to 63, all different within a row
- gate_values: float32 [32768, 2], P('expert'), may hold values from 0.2 to 1
- w_up: bfloat16 [64, 1664, 4096], P('expert', None, 'tensor'), may hold values from -0.15625 to 0.15625
- w_down: bfloat16 [64, 4096, 1664], P('expert', 'tensor'), may hold values from -0.09375 to 0.09375
Outputs:
- mixed: bfloat16 [32768, 1664], P('expert', 'tensor')
Inputs may be any that keep to these rules, and one draw needn't show every extreme that they name: `expert_ids`: the 2 experts of a patch differ, and every expert is chosen by some patch.
All inputs are finite; a program needn't handle non-finite values.
Results may differ from a plain program's by a relative error of at most 0.019.
Values may be sent and summed in bfloat16 or wider, within the bound.
A program may use at most 128 MiB of HBM per device.

v0:
```python
import jax
import jax.numpy as jnp
from jax import lax
from jax.sharding import PartitionSpec as P

TOP = 2


def slot_targets(expert_ids, experts, capacity):
    count = expert_ids.shape[0]
    onehot = (expert_ids[:, :, None] == jnp.arange(experts, dtype=jnp.int32)).astype(jnp.int32)
    ordered = jnp.transpose(onehot, (1, 0, 2)).reshape(TOP * count, experts)
    before = jnp.cumsum(ordered, axis=0) - ordered
    rank = jnp.sum(before * ordered, axis=1).reshape(TOP, count).T
    target = expert_ids * capacity + rank
    return jnp.where(rank < capacity, target, experts * capacity)


def place_rows(rows, target, experts, capacity):
    width = rows.shape[1]
    copies = jnp.broadcast_to(rows[:, None, :], (rows.shape[0], TOP, width)).reshape(-1, width)
    filled = (
        jnp.zeros((experts * capacity, width), jnp.bfloat16)
        .at[target.reshape(-1)]
        .set(copies, mode="drop")
    )
    return filled.reshape(experts, capacity, width)


def group_terms(rows, up_weight, down_weight):
    sources, slots, width = rows.shape
    flat = rows.reshape(sources * slots, width)
    hidden = jax.nn.gelu(
        jnp.dot(flat, up_weight, preferred_element_type=jnp.float32), approximate=False
    ).astype(jnp.bfloat16)
    term = jnp.dot(hidden, down_weight, preferred_element_type=jnp.float32).astype(jnp.bfloat16)
    return term.reshape(sources, slots, width)


def local(patches, expert_ids, gate_values, w_up, w_down):
    experts = lax.axis_size("expert")
    count = patches.shape[0]
    capacity = 21 * TOP * count // (20 * experts)
    target = slot_targets(expert_ids, experts, capacity)
    up_weight = w_up[0]
    down_weight = w_down[0]
    whole = lax.all_gather(patches, "tensor", axis=1, tiled=True)
    outgoing = place_rows(whole, target, experts, capacity)
    terms = group_terms(
        lax.all_to_all(outgoing, "expert", split_axis=0, concat_axis=0, tiled=True),
        up_weight,
        down_weight,
    )
    returned = lax.all_to_all(terms, "expert", split_axis=0, concat_axis=0, tiled=True)
    summed = lax.psum_scatter(
        returned.astype(jnp.float32).astype(jnp.bfloat16), "tensor", scatter_dimension=2, tiled=True
    )
    flat_out = summed.reshape(experts * capacity, summed.shape[2])
    total = jnp.zeros((count, flat_out.shape[1]), jnp.float32)
    for choice_index in range(TOP):
        values = jnp.take(flat_out, target[:, choice_index], axis=0, mode="fill", fill_value=0)
        total = total + gate_values[:, choice_index][:, None] * values.astype(jnp.float32)
    return total.astype(jnp.bfloat16)


def solution(mesh):
    in_specs = (
        P("expert", "tensor"),
        P("expert", None),
        P("expert", None),
        P("expert", None, "tensor"),
        P("expert", "tensor", None),
    )
    out_specs = P("expert", "tensor")
    return jax.shard_map(local, mesh=mesh, in_specs=in_specs, out_specs=out_specs, check_vma=False)
```

profile of v0, /device:TPU:1, one launch (start us, length us, event | category | flops | bytes accessed | tf_op | source)
XLA Modules:
  0.0 400.9 jit_solution(11003732196126051022)
XLA Ops:
  6.5 0.0 copy-start
  6.5 0.0 copy-start.1
  6.5 0.0 all-gather.2.cloned.1.call-start
  6.5 0.7 all-gather.2.cloned.1.call-update
  7.3 0.0 reduce-scatter.4.cloned.1.call-start
  7.3 0.7 eq.34
  8.0 18.0 %reduce-window.6 = s32[64,8,128]{2,1,0:T(8,128)S(1)} reduce-window(s32[64,8,128]{2,1,0:T(8,128)S(1)} %fusion.52, s32[]{:T(128)} %constant.43.clone.1), window={size=1x1x128 pad=0_0x0_0x127_0}, to_apply=%region_0.0 | reduce-window | flops 8323072 | bytes 524292 | tf_op jit(solution)/shard_map/reduce-window
  26.0 0.1 slice.28
  26.2 0.1 copy.13
  26.4 0.1 copy.14
  26.4 0.7 copy.20
  27.1 0.1 broadcast_add_fusion
  27.3 0.1 fusion.51
  27.4 0.0 copy-done.1
  27.4 0.1 copy.15
  27.5 0.2 reshape.74
  27.7 17.7 %all-gather.2.cloned.1.call-done = bf16[512,1664]{0,1:T(8,128)(2,1)} async-done(((bf16[512,208]{0,1:T(8,128)(2,1)}), bf16[512,1664]{0,1:T(8,128)(2,1)}) %all-gather.2.cloned.1.call-update) | async-done | bytes 1703952 | tf_op jit(solution)/shard_map/all_gather | solution.py:47
  45.5 2.7 copy.16
  48.2 6.4 %broadcast_in_dim.27 = bf16[512,2,1664]{2,1,0:T(2,128)(2,1)} broadcast(bf16[512,1664]{1,0:T(8,128)(2,1)S(1)} %copy.16), dimensions={0,2} | broadcast | bytes 5111808 | tf_op jit(solution)/shard_map/broadcast_in_dim | solution.py:21
  54.6 8.1 %reshape.100 = bf16[1024,1664]{1,0:T(8,128)(2,1)} reshape(bf16[512,2,1664]{2,1,0:T(2,128)(2,1)} %broadcast_in_dim.27) | data formatting | bytes 6815744 | tf_op jit(solution)/shard_map/reshape | solution.py:21
  62.8 8.8 %scatter_custom_fusion = bf16[1024,1664]{1,0:T(8,128)(2,1)} fusion(s32[1024]{0:T(1024)S(1)} %bitcast.66, bf16[1024,1664]{1,0:T(8,128)(2,1)} %reshape.100, bf16[]{:T(256)} %constant.42.clone.1), kind=kCustom, calls=%fused_computation.26 | custom fusion | bytes 3408384 | tf_op jit(solution)/shard_map/scatter | solution.py:25
  71.5 0.0 copy-start.3
  71.5 90.6 %all_to_all.10 = bf16[64,16,1664]{2,1,0:T(8,128)(2,1)} all-to-all(bf16[64,16,1664]{2,1,0:T(8,128)(2,1)} %bitcast.51), channel_id=1, replica_groups=mesh['expert'=64,'tensor'=8] {'expert'}, dimensions={0} | all-to-all | bytes 6815744 | tf_op jit(solution)/shard_map/all_to_all | solution.py:50
  162.2 0.0 copy-done
  162.2 0.0 copy-done.3
  162.2 11.1 %convolution_convert_fusion = bf16[1024,1664]{1,0:T(8,128)(2,1)} fusion(bf16[1,512,1664]{2,1,0:T(8,128)(2,1)S(1)} %copy-done, bf16[1024,1664]{1,0:T(8,128)(2,1)} %bitcast.53, bf16[1,1664,512]{2,1,0:T(8,128)(2,1)S(1)} %copy-done.3), kind=kOutput, calls=%fused_computation.3 | convolution fusion | flops 3525443584 | bytes 10223616 | tf_op jit(solution)/shard_map/dot_general | solution.py:36
  173.3 93.0 %all_to_all.11 = bf16[64,16,1664]{2,1,0:T(8,128)(2,1)} all-to-all(bf16[64,16,1664]{2,1,0:T(8,128)(2,1)} %bitcast.54), channel_id=1, replica_groups=mesh['expert'=64,'tensor'=8] {'expert'}, dimensions={0} | all-to-all | bytes 6815744 | tf_op jit(solution)/shard_map/all_to_all | solution.py:54
  266.3 25.3 %copy.18 = bf16[64,16,1664]{1,0,2:T(8,128)(2,1)} copy(bf16[64,16,1664]{2,1,0:T(8,128)(2,1)} %all_to_all.11) | data formatting | bytes 6815744
  291.5 47.2 %reshape.110 = bf16[1664,1024]{1,0:T(8,128)(2,1)} reshape(bf16[1664,64,16]{2,1,0:T(8,128)(2,1)} %bitcast.48) | data formatting | bytes 6815744
  338.7 0.0 copy-start.2
  338.7 0.0 reduce-scatter.4.cloned.1.call-update
  338.9 0.6 copy-done.2
  339.4 40.9 %reduce-scatter.4.cloned.1.call-done = bf16[208,1024]{1,0:T(8,128)(2,1)} async-done(((bf16[1664,1024]{1,0:T(8,128)(2,1)}), bf16[208,1024]{1,0:T(8,128)(2,1)}) %reduce-scatter.4.cloned.1.call-update) | async-done | bytes 426000
  380.3 4.7 %reshape.111 = bf16[208,64,16]{2,1,0:T(8,128)(2,1)} reshape(bf16[208,1024]{1,0:T(8,128)(2,1)} %reduce-scatter.4.cloned.1.call-done) | data formatting | bytes 851968
  385.1 3.9 copy.19
  389.0 2.0 gather_fusion.1
  391.0 2.0 gather_fusion
  392.9 0.3 add_convert_fusion
  393.3 0.8 copy.17
  (13 shorter events, 0.1 us)
Async XLA Ops:
  6.5 155.6 %copy-start = (bf16[1,512,1664]{2,1,0:T(8,128)(2,1)S(1)}, bf16[1,512,1664]{2,1,0:T(8,128)(2,1)}, u32[]{:S(2)}) copy-start(bf16[1,512,1664]{2,1,0:T(8,128)(2,1)} %param.11) | copy-start | bytes 5111812
  6.5 20.8 %copy-start.1 = (s32[512,2]{0,1:T(2,128)S(1)}, s32[512,2]{0,1:T(2,128)}, u32[]{:S(2)}) copy-start(s32[512,2]{0,1:T(2,128)} %param.8) | copy-start | bytes 12292
  6.5 38.9 %all-gather.2.cloned.1.call-start = ((), (), s32[]{:S(2)}) async-start(), calls=%async_computation.3 | async-start | bytes 1916928 | tf_op jit(solution)/shard_map/all_gather | solution.py:47
  7.3 373.1 %reduce-scatter.4.cloned.1.call-start = ((), (), s32[]{:S(2)}) async-start(), calls=%async_computation.4 | async-start | bytes 3833856
  71.5 90.6 %copy-start.3 = (bf16[1,1664,512]{2,1,0:T(8,128)(2,1)S(1)}, bf16[1,1664,512]{2,1,0:T(8,128)(2,1)}, u32[]{:S(2)}) copy-start(bf16[1,1664,512]{2,1,0:T(8,128)(2,1)} %param.10) | copy-start | bytes 5111812
  338.7 0.7 copy-start.2
Sparse Core Ops, SparseCore 0:
  9.5 35.9 all-gather.1
  338.9 41.4 reduce-scatter.3
where the time goes:
time: 403 us; the launch traced here: 401 us
  blocking collectives  184 us (46%)
  local copies, waits for them, and re-layouts  115 us (29%)
  waiting for transfers between devices  59.4 us (15%)
  other arithmetic  18.6 us (5%)
  between operations  13.6 us (3%)
  matrix products  11.1 us (3%)
    all_to_all x1, blocking collectives, local(): lax.all_to_all(terms, 'expert', split_axis=0, concat_axis=0, tiled=True)  93 us
    all_to_all x1, blocking collectives, local(): lax.all_to_all(outgoing, 'expert', split_axis=0, concat_axis=0, tiled=True)  90.6 us
    unnamed x13, local copies, waits for them, and re-layouts  82.4 us
    unnamed x3, waiting for transfers between devices  41.6 us
    another operation x3, other arithmetic  18.2 us
    all_gather x1, waiting for transfers between devices, local(): whole = lax.all_gather(patches, 'tensor', axis=1, tiled=True)  17.7 us
    dot_general x1, matrix products, group_terms(): jnp.dot(hidden, down_weight, preferred_element_type=jnp.float32)  11.1 us
    scatter x1, local copies, waits for them, and re-layouts, place_rows(): filled = jnp.zeros((experts * capacity, width), jnp.bfloat16).at[target.r...  8.79 us
  transfers between devices with their start and end apart: 2, of which 2 were waited for; matrix products, arithmetic and copies ran while one was open for 5% of the time, Pallas kernels for 0%

commit v1 on v0

v1 whole, which is shorter than its diff:
```python
import functools

import jax
import jax.numpy as jnp
from jax import lax
from jax.experimental import pallas as pl
from jax.experimental.pallas import tpu as pltpu
from jax.sharding import PartitionSpec as P

TOP = 2
CHUNKS = 4
MESH = pl.DeviceIdType.MESH
BF16 = jnp.bfloat16
F32 = jnp.float32

OWN_R, OWN_L, FWD_R, FWD_L, SIB_OWN, SIB_L, SIB_R, SIB_FA, SIB_FB = range(9)
SIB_SUM, HALF_R, HALF_L, SUM_R, SUM_L = range(9, 14)
KINDS = 14


def erf(x):
    x = jnp.clip(x, -3.832506856900711, 3.832506856900711)
    s = x * x
    num = jnp.full_like(s, 0.00022905065861350646)
    for coef in (0.0034082910107109506, 0.050955695062380861, 0.18520832239976145, 1.128379143519084):
        num = num * s + coef
    den = jnp.full_like(s, -1.1791602954361697e-7)
    for coef in (0.000023547966471313185, 0.0010179625278914885, 0.014070470171167667, 0.11098505178285362, 0.49746925110067538, 1.0):
        den = den * s + coef
    return x * num / den


def gelu(x):
    return 0.5 * x * (1.0 + erf(x * 0.7071067811865476))


def layer_kernel(
    dims,
    patches_ref, ids_ref, gates_ref, up_hbm, down_hbm,
    out_ref,
    up_v, down_v, up_t, down_t, padded, onehot, send, rows_in, feats,
    other, from_sib, own, sums, half_l, half_r, full_l, full_r, back, rows_out,
    w_sem, a2a_send, a2a_recv, back_send, back_recv, send_sem, recv_sem,
):
    ny, nz, nt, cap, dsh, chunks = dims
    experts = ny * nz
    nx = nt // 2
    count = ids_ref.shape[1]
    slots = experts * cap
    per = experts // chunks
    repeat = per // ny
    lanes = per * cap
    width = send.shape[1]
    cut = (dsh // 16 + 1) // 2 * 16

    e = lax.axis_index("expert")
    t = lax.axis_index("tensor")
    y, z = e // nz, e % nz
    x, core = t // 2, t % 2
    right = (t + 2) % nt
    left = (t + nt - 2) % nt
    sib = x * 2 + 1 - core

    def shard_of(step, parity):
        return ((x + step) % nx) * 2 + parity

    def shift(k):
        chunk, i = k // per, k % per
        dy = i // repeat
        dz = (chunk + chunks * (i % repeat) + ny * nz - dy) % nz
        return dy, dz

    def block(at):
        return pl.ds(pl.multiple_of(at * cap, cap), cap)

    up_copy = pltpu.make_async_copy(up_hbm, up_v, w_sem.at[0])
    down_copy = pltpu.make_async_copy(down_hbm, down_v, w_sem.at[1])
    up_copy.start()
    down_copy.start()

    barrier = pltpu.get_barrier_semaphore()

    def greet(k, carry):
        pl.semaphore_signal(barrier, inc=1, device_id={"expert": (e + k) % experts}, device_id_type=MESH)
        return carry

    lax.fori_loop(1, experts, greet, 0)
    for partner in (right, left, sib):
        pl.semaphore_signal(barrier, inc=1, device_id={"tensor": partner}, device_id_type=MESH)

    padded[...] = jnp.zeros_like(padded)
    padded[0:dsh, :] = patches_ref[...]
    earlier = (
        lax.broadcasted_iota(jnp.int32, (count, count), 0) < lax.broadcasted_iota(jnp.int32, (count, count), 1)
    ).astype(F32).astype(BF16)
    expert_row = lax.broadcasted_iota(jnp.int32, (experts, count), 0)
    targets = []
    taken = jnp.zeros((experts, 1), F32)
    for k in range(TOP):
        ids = ids_ref[k:k + 1, :]
        hot = (expert_row == ids).astype(F32)
        before = jnp.dot(hot.astype(BF16), earlier, preferred_element_type=F32) + taken
        rank = jnp.sum(hot * before, axis=0, keepdims=True)
        taken = taken + jnp.sum(hot, axis=1, keepdims=True)
        targets.append(jnp.where(rank < cap, ids.astype(F32) * cap + rank, -1.0))

    tile = min(256, slots)

    def place(i, carry):
        at = pl.ds(pl.multiple_of(i * tile, tile), tile)
        slot = (lax.broadcasted_iota(jnp.int32, (tile, count), 0) + i * tile).astype(F32)
        both = jnp.zeros((tile, count), F32)
        for k in range(TOP):
            hit = (slot == targets[k]).astype(F32)
            onehot[k, at, :] = hit.astype(BF16)
            both = both + hit
        send[at, :] = lax.dot_general(
            both.astype(BF16), padded[...], (((1,), (1,)), ((), ())), preferred_element_type=F32
        ).astype(BF16)
        return carry

    lax.fori_loop(0, slots // tile, place, 0)

    pl.semaphore_wait(barrier, experts - 1 + 3)

    def out_copy(k):
        dy, dz = shift(k)
        to = ((y + dy) % ny) * nz + (z + dz) % nz
        return pltpu.make_async_remote_copy(
            src_ref=send.at[block(to)], dst_ref=rows_in.at[block(k)],
            send_sem=a2a_send, recv_sem=a2a_recv.at[k // per],
            device_id={"expert": to}, device_id_type=MESH,
        )

    def back_copy(k):
        dy, dz = shift(k)
        to = ((y + ny - dy) % ny) * nz + (z + nz - dz) % nz
        return pltpu.make_async_remote_copy(
            src_ref=back.at[block(k)], dst_ref=rows_out.at[block(e)],
            send_sem=back_send, recv_sem=back_recv,
            device_id={"expert": to}, device_id_type=MESH,
        )

    def send_out(k, carry):
        out_copy(k).start()
        return carry

    lax.fori_loop(1, experts, send_out, 0)
    rows_in[0:cap, :] = send[block(e), :]

    up_copy.wait()
    up_t[...] = up_v[...].T
    down_copy.wait()
    down_t[...] = down_v[...].T

    def shard(step, parity, first=0, size=None):
        size = dsh if size is None else size
        return pl.ds(pl.multiple_of(shard_of(step, parity) * dsh + first, 16), size)

    def push(kind, c, src, dst, partner):
        return pltpu.make_async_remote_copy(
            src_ref=src, dst_ref=dst, send_sem=send_sem.at[kind, c], recv_sem=recv_sem.at[kind, c],
            device_id={"tensor": partner}, device_id_type=MESH,
        )

    def gather_copy(kind, c):
        step, first, size, partner = {
            OWN_R: (0, 0, dsh, right),
            OWN_L: (0, 0, dsh, left),
            FWD_R: (nx - 1, 0, cut, right),
            FWD_L: (1, cut, dsh - cut, left),
            SIB_OWN: (0, 0, dsh, sib),
            SIB_L: (nx - 1, 0, dsh, sib),
            SIB_R: (1, 0, dsh, sib),
            SIB_FA: (2, 0, cut, sib),
            SIB_FB: (2, cut, dsh - cut, sib),
        }[kind]
        ref = feats.at[c, shard(step, core, first, size)]
        return push(kind, c, ref, ref, partner)

    def sum_copy(kind, c):
        if kind == SIB_SUM:
            return push(kind, c, other.at[c], from_sib.at[c], sib)
        if kind == HALF_R:
            return push(kind, c, sums.at[c, 2, pl.ds(0, cut)], half_l.at[c], right)
        if kind == HALF_L:
            return push(kind, c, sums.at[c, 2, pl.ds(cut, dsh - cut)], half_r.at[c], left)
        if kind == SUM_R:
            return push(kind, c, sums.at[c, 1], full_l.at[c], right)
        return push(kind, c, sums.at[c, nx - 1], full_r.at[c], left)

    def chunk_rows(c):
        return pl.ds(pl.multiple_of(c * lanes, lanes), lanes)

    def arrive(c):
        @pl.when(c == 0)
        def _():
            ref = rows_in.at[pl.ds(cap, lanes - cap)]
            pltpu.make_async_copy(ref, ref, a2a_recv.at[0]).wait()

        @pl.when(c > 0)
        def _():
            ref = rows_in.at[chunk_rows(c)]
            pltpu.make_async_copy(ref, ref, a2a_recv.at[c]).wait()

        turned = rows_in[chunk_rows(c), :].T
        feats[c, shard(0, core), :] = turned[0:dsh, :]
        for kind in (OWN_R, OWN_L, SIB_OWN):
            gather_copy(kind, c).start()

    def forward(c):
        gather_copy(OWN_R, c).wait_recv()
        gather_copy(FWD_R, c).start()
        gather_copy(SIB_L, c).start()
        gather_copy(OWN_L, c).wait_recv()
        gather_copy(FWD_L, c).start()
        gather_copy(SIB_R, c).start()

    def forward_last(c):
        gather_copy(FWD_R, c).wait_recv()
        gather_copy(SIB_FA, c).start()
        gather_copy(FWD_L, c).wait_recv()
        gather_copy(SIB_FB, c).start()

    def compute(c):
        for kind in (SIB_OWN, SIB_L, SIB_R, SIB_FA, SIB_FB):
            gather_copy(kind, c).wait_recv()
        hidden = gelu(jnp.dot(up_t[...], feats[c], preferred_element_type=F32)).astype(BF16)
        for step in range(nx):
            other[c, step] = jnp.dot(
                down_t[shard(step, 1 - core), :], hidden, preferred_element_type=F32
            ).astype(BF16)
        sum_copy(SIB_SUM, c).start()
        for step in range(nx):
            own[c, step] = jnp.dot(down_t[shard(step, core), :], hidden, preferred_element_type=F32)

    def add_sibling(c):
        sum_copy(SIB_SUM, c).wait_recv()
        sums[c, 2] = (own[c, 2] + from_sib[c, 2].astype(F32)).astype(BF16)
        sum_copy(HALF_R, c).start()
        sum_copy(HALF_L, c).start()
        for step in (0, 1, nx - 1):
            own[c, step] = own[c, step] + from_sib[c, step].astype(F32)

    def add_half(c):
        sum_copy(HALF_R, c).wait_recv()
        sums[c, 1, 0:cut] = (own[c, 1, 0:cut] + half_l[c].astype(F32)).astype(BF16)
        sums[c, 1, cut:dsh] = own[c, 1, cut:dsh].astype(BF16)
        sum_copy(SUM_R, c).start()
        sum_copy(HALF_L, c).wait_recv()
        sums[c, nx - 1, 0:cut] = own[c, nx - 1, 0:cut].astype(BF16)
        sums[c, nx - 1, cut:dsh] = (own[c, nx - 1, cut:dsh] + half_r[c].astype(F32)).astype(BF16)
        sum_copy(SUM_L, c).start()

    def finish(c):
        sum_copy(SUM_R, c).wait_recv()
        sum_copy(SUM_L, c).wait_recv()
        done = own[c, 0] + full_l[c].astype(F32) + full_r[c].astype(F32)
        if width > dsh:
            done = jnp.concatenate([done, jnp.zeros((width - dsh, lanes), F32)], axis=0)
        back[chunk_rows(c), :] = done.astype(BF16).T

        def give_back(i, carry):
            k = c * per + i

            @pl.when(k > 0)
            def _():
                back_copy(k).start()

            return carry

        lax.fori_loop(0, per, give_back, 0)

    stages = (arrive, forward, forward_last, compute, add_sibling, add_half, finish)

    def step(at, carry):
        for index, stage in enumerate(stages):
            c = at - index
            pl.when((c >= 0) & (c < chunks))(functools.partial(stage, c))
        return carry

    lax.fori_loop(0, chunks + len(stages) - 1, step, 0)

    rows_out[block(e), :] = back[0:cap, :]
    for c in range(chunks):
        for kind in range(SIB_SUM):
            gather_copy(kind, c).wait_send()
        for kind in range(SIB_SUM, KINDS):
            sum_copy(kind, c).wait_send()
    rest = pl.ds(0, slots - cap)
    pltpu.make_async_copy(send.at[rest], send.at[rest], a2a_send).wait()
    pltpu.make_async_copy(back.at[rest], back.at[rest], back_send).wait()
    pltpu.make_async_copy(rows_out.at[rest], rows_out.at[rest], back_recv).wait()

    turned = rows_out[...].T[0:dsh, :]
    total = jnp.zeros((dsh, count), F32)
    for k in range(TOP):
        total = total + gates_ref[k:k + 1, :] * jnp.dot(turned, onehot[k], preferred_element_type=F32)
    out_ref[...] = total.astype(BF16)


def local(patches, expert_ids, gate_values, w_up, w_down):
    experts = lax.axis_size("expert")
    nt = lax.axis_size("tensor")
    count, dsh = patches.shape
    width = (dsh + 127) // 128 * 128
    model, hid = w_up.shape[1:]
    cap = 21 * TOP * count // (20 * experts)
    slots = experts * cap
    ny = next(n for n in range(1, experts + 1) if n * n >= experts)
    nz = experts // ny
    chunks = min(CHUNKS, nz)
    lanes = slots // chunks
    nx = nt // 2
    cut = (dsh // 16 + 1) // 2 * 16
    vmem = pl.BlockSpec(memory_space=pltpu.VMEM)
    hbm = pl.BlockSpec(memory_space=pl.ANY)
    dma = pltpu.SemaphoreType.DMA
    mixed = pl.pallas_call(
        functools.partial(layer_kernel, (ny, nz, nt, cap, dsh, chunks)),
        out_shape=jax.ShapeDtypeStruct((dsh, count), BF16),
        in_specs=[vmem, vmem, vmem, hbm, hbm],
        out_specs=vmem,
        scratch_shapes=[
            pltpu.VMEM((model, hid), BF16),
            pltpu.VMEM((hid, model), BF16),
            pltpu.VMEM((hid, model), BF16),
            pltpu.VMEM((model, hid), BF16),
            pltpu.VMEM((width, count), BF16),
            pltpu.VMEM((TOP, slots, count), BF16),
            pltpu.VMEM((slots, width), BF16),
            pltpu.VMEM((slots, width), BF16),
            pltpu.VMEM((chunks, model, lanes), BF16),
            pltpu.VMEM((chunks, nx, dsh, lanes), BF16),
            pltpu.VMEM((chunks, nx, dsh, lanes), BF16),
            pltpu.VMEM((chunks, nx, dsh, lanes), F32),
            pltpu.VMEM((chunks, nx, dsh, lanes), BF16),
            pltpu.VMEM((chunks, cut, lanes), BF16),
            pltpu.VMEM((chunks, dsh - cut, lanes), BF16),
            pltpu.VMEM((chunks, dsh, lanes), BF16),
            pltpu.VMEM((chunks, dsh, lanes), BF16),
            pltpu.VMEM((slots, width), BF16),
            pltpu.VMEM((slots, width), BF16),
            dma((2,)),
            dma,
            dma((chunks,)),
            dma,
            dma,
            dma((KINDS, chunks)),
            dma((KINDS, chunks)),
        ],
        compiler_params=pltpu.CompilerParams(
            collective_id=0, has_side_effects=True, vmem_limit_bytes=50 * 1024 * 1024
        ),
        cost_estimate=pl.CostEstimate(
            flops=4 * slots * model * hid, bytes_accessed=4 * model * hid, transcendentals=0
        ),
    )(patches.T, expert_ids.T, gate_values.T, w_up[0], w_down[0])
    return mixed.T


def solution(mesh):
    in_specs = (
        P("expert", "tensor"),
        P("expert", None),
        P("expert", None),
        P("expert", None, "tensor"),
        P("expert", "tensor", None),
    )
    out_specs = P("expert", "tensor")
    return jax.shard_map(local, mesh=mesh, in_specs=in_specs, out_specs=out_specs, check_vma=False)
```

time: 403 us -> 78.9 us (0.20)
  the two profiles are of different devices: /device:TPU:1 before, /device:TPU:8 now
where the time goes in v1:
time: 78.9 us; the launch traced here: 78.6 us
  Pallas kernels  72.7 us (92%)
  local copies, waits for them, and re-layouts  5.9 us (7%)
    pallas_call x1, Pallas kernels, local(): pl.pallas_call(functools.partial(layer_kernel, (ny, nz, nt, cap, dsh, chu...  72.7 us
    unnamed x11, local copies, waits for them, and re-layouts  5.9 us

profile of v1, /device:TPU:8, one launch (start us, length us, event | category | flops | bytes accessed | tf_op | source)
XLA Modules:
  0.0 78.6 jit_solution(15076247799234419061)
XLA Ops:
  0.0 0.0 copy-start
  0.0 1.5 %copy-done = bf16[1,1664,512]{2,1,0:T(8,128)(2,1)S(1)} copy-done((bf16[1,1664,512]{2,1,0:T(8,128)(2,1)S(1)}, bf16[1,1664,512]{2,1,0:T(8,128)(2,1)}, u32[]{:S(2)}) %copy-start) | copy-done | bytes 1703960
  1.5 0.0 copy-start.1
  1.5 1.5 %copy-done.1 = bf16[1,512,1664]{2,1,0:T(8,128)(2,1)S(1)} copy-done((bf16[1,512,1664]{2,1,0:T(8,128)(2,1)S(1)}, bf16[1,512,1664]{2,1,0:T(8,128)(2,1)}, u32[]{:S(2)}) %copy-start.1) | copy-done | bytes 1703960
  2.9 0.0 copy-start.2
  2.9 0.9 %copy-done.2 = bf16[512,208]{0,1:T(8,128)(2,1)S(1)} copy-done((bf16[512,208]{0,1:T(8,128)(2,1)S(1)}, bf16[512,208]{0,1:T(8,128)(2,1)}, u32[]{:S(2)}) %copy-start.2) | copy-done | bytes 213016
  3.8 0.0 copy-start.3
  3.8 0.7 copy-done.3
  4.5 0.0 copy-start.4
  4.5 0.7 copy-done.4
  5.2 72.7 %shard_map.55 = bf16[208,512]{1,0:T(8,128)(2,1)S(1)} custom-call(bf16[208,512]{1,0:T(8,128)(2,1)S(1)} %bitcast.9, s32[2,512]{1,0:T(2,128)S(1)} %bitcast.10, f32[2,512]{1,0:T(2,128)S(1)} %bitcast.11, bf16[1664,512]{1,0:T(8,128)(2,1)S(1)} %bitcast.7, bf16[512,1664]{1,0:T(8,128)(2,1)S(1)} %bitcast.8), custom_call_target="tpu_custom_call" | custom-call | flops 3489660928 | bytes 3407872 | tf_op jit(solution)/shard_map/pallas_call | solution.py:319
  77.9 0.7 copy.7
Async XLA Ops:
  0.0 1.5 %copy-start = (bf16[1,1664,512]{2,1,0:T(8,128)(2,1)S(1)}, bf16[1,1664,512]{2,1,0:T(8,128)(2,1)}, u32[]{:S(2)}) copy-start(bf16[1,1664,512]{2,1,0:T(8,128)(2,1)} %param.8) | copy-start | bytes 5111812
  1.5 1.5 %copy-start.1 = (bf16[1,512,1664]{2,1,0:T(8,128)(2,1)S(1)}, bf16[1,512,1664]{2,1,0:T(8,128)(2,1)}, u32[]{:S(2)}) copy-start(bf16[1,512,1664]{2,1,0:T(8,128)(2,1)} %param.9) | copy-start | bytes 5111812
  2.9 0.9 %copy-start.2 = (bf16[512,208]{0,1:T(8,128)(2,1)S(1)}, bf16[512,208]{0,1:T(8,128)(2,1)}, u32[]{:S(2)}) copy-start(bf16[512,208]{0,1:T(8,128)(2,1)} %param.5) | copy-start | bytes 638980
  3.8 0.7 copy-start.3
  4.5 0.7 copy-start.4

commit v2 on v1

v2 whole, which is shorter than its diff:
```python
import functools

import jax
import jax.numpy as jnp
from jax import lax
from jax.experimental import pallas as pl
from jax.experimental.pallas import tpu as pltpu
from jax.sharding import PartitionSpec as P

TOP = 2
VMEM_LIMIT = 60 * 1024 * 1024
MESH = pl.DeviceIdType.MESH
BF16 = jnp.bfloat16
F32 = jnp.float32

OWN_RA, OWN_RB, OWN_LA, OWN_LB, FWD_R, FWD_L, SIB_OWN, SIB_L, SIB_R, SIB_FA, SIB_FB = range(11)
SIB_HID, HALF_R, HALF_L, SUM_RA, SUM_RB, SUM_LA, SUM_LB, SIB_DOWN = range(11, 19)
KINDS = 19

GATHER = (2, 2, 2, 2)
HIDDEN = (2, 2, 2, 2)
RETURN = (2, 2, 2, 2)
ORDER = (
    ("A", 0), ("A", 1), ("F", 0), ("F", 1), ("A", 2), ("L", 0),
    ("A", 3), ("L", 1), ("U", 0), ("F", 2), ("U", 1), ("F", 3),
    ("D", 0), ("L", 2), ("D", 1), ("U", 2), ("L", 3), ("H", 0),
    ("D", 2), ("H", 1), ("U", 3), ("E", 0), ("H", 2), ("D", 3),
    ("E", 1), ("E", 2), ("H", 3), ("E", 3),
)


def gelu(x):
    return 0.5 * x * (1.0 + lax.erf(x * 0.7071067811865476))


def pieces_of(sizes):
    starts = [sum(sizes[:i]) for i in range(len(sizes))]
    return list(zip(starts, sizes))


def plan(groups):
    if groups == sum(GATHER):
        return GATHER, HIDDEN, RETURN, ORDER
    ones = (1,) * groups
    return ones, ones, ones, tuple((op, at) for at in range(groups) for op in "AFLUDHE")


def layer_kernel(
    dims, pieces, order,
    patches_hbm, ids_hbm, gates_hbm, up_hbm, down_hbm,
    out_ref,
    patches_v, ids_v, gates_v, up_v, down_v, up_t, down_t, down_all,
    onehot, send, rows_in, feats, hid, acc, sums, half_l, half_r, full_l, full_r, back, rows_out,
    in_sem, a2a_send, a2a_recv, back_send, back_recv, send_sem, recv_sem,
):
    ny, nz, nt, cap, dsh, hidden = dims
    gather_at, hidden_at, return_at = pieces
    experts = ny * nz
    nx = nt // 2
    count = ids_v.shape[1]
    slots = experts * cap
    unit = ny * cap
    width = send.shape[1]
    cut = (dsh // 16 + 1) // 2 * 16

    e = lax.axis_index("expert")
    t = lax.axis_index("tensor")
    y, z = e // nz, e % nz
    x, core = t // 2, t % 2
    right = (t + 2) % nt
    left = (t + nt - 2) % nt
    sib = x * 2 + 1 - core

    loads = [
        pltpu.make_async_copy(src, dst, in_sem.at[i])
        for i, (src, dst) in enumerate((
            (ids_hbm, ids_v), (patches_hbm, patches_v.at[pl.ds(0, dsh)]), (gates_hbm, gates_v),
            (up_hbm, up_v), (down_hbm, down_v),
        ))
    ]
    for load in loads[:2]:
        load.start()

    barrier = pltpu.get_barrier_semaphore()

    def greet(k, carry):
        pl.semaphore_signal(barrier, inc=1, device_id={"expert": (e + k) % experts}, device_id_type=MESH)
        return carry

    lax.fori_loop(1, experts, greet, 0)
    for partner in (right, left, sib):
        pl.semaphore_signal(barrier, inc=1, device_id={"tensor": partner}, device_id_type=MESH)

    for load in loads[2:]:
        load.start()

    def shard_of(step, parity):
        return ((x + step) % nx) * 2 + parity

    def shift(k):
        dy = k % ny
        dz = (k // ny + ny * nz - dy) % nz
        return dy, dz

    def block(at):
        return pl.ds(pl.multiple_of(at * cap, cap), cap)

    def lanes(piece):
        start, size = piece
        return pl.ds(start * unit, size * unit)

    if width > dsh:
        patches_v[dsh:width, :] = jnp.zeros((width - dsh, count), BF16)
    earlier = (
        lax.broadcasted_iota(jnp.int32, (count, count), 0) < lax.broadcasted_iota(jnp.int32, (count, count), 1)
    ).astype(F32).astype(BF16)
    expert_row = lax.broadcasted_iota(jnp.int32, (experts, count), 0)
    targets = []
    taken = jnp.zeros((experts, 1), F32)
    loads[0].wait()
    for k in range(TOP):
        ids = ids_v[k:k + 1, :]
        hot = (expert_row == ids).astype(F32)
        before = jnp.dot(hot.astype(BF16), earlier, preferred_element_type=F32) + taken
        rank = jnp.sum(hot * before, axis=0, keepdims=True)
        taken = taken + jnp.sum(hot, axis=1, keepdims=True)
        targets.append(jnp.where(rank < cap, ids.astype(F32) * cap + rank, -1.0))
    loads[1].wait()

    tile = min(256, slots)

    def place(i, carry):
        at = pl.ds(pl.multiple_of(i * tile, tile), tile)
        slot = (lax.broadcasted_iota(jnp.int32, (tile, count), 0) + i * tile).astype(F32)
        both = jnp.zeros((tile, count), F32)
        for k in range(TOP):
            hit = (slot == targets[k]).astype(F32)
            onehot[k, at, :] = hit.astype(BF16)
            both = both + hit
        send[at, :] = lax.dot_general(
            both.astype(BF16), patches_v[...], (((1,), (1,)), ((), ())), preferred_element_type=F32
        ).astype(BF16)
        return carry

    lax.fori_loop(0, slots // tile, place, 0)

    pl.semaphore_wait(barrier, experts - 1 + 3)

    for index, (start, size) in enumerate(gather_at):
        def send_out(k, carry, index=index):
            dy, dz = shift(k)
            to = ((y + dy) % ny) * nz + (z + dz) % nz
            pltpu.make_async_remote_copy(
                src_ref=send.at[block(to)], dst_ref=rows_in.at[block(k)],
                send_sem=a2a_send, recv_sem=a2a_recv.at[index],
                device_id={"expert": to}, device_id_type=MESH,
            ).start()
            return carry

        lax.fori_loop(max(1, start * ny), (start + size) * ny, send_out, 0)
    rows_in[0:cap, :] = send[block(e), :]

    def push(kind, c, src, dst, partner):
        return pltpu.make_async_remote_copy(
            src_ref=src, dst_ref=dst, send_sem=send_sem.at[kind, c], recv_sem=recv_sem.at[kind, c],
            device_id={"tensor": partner}, device_id_type=MESH,
        )

    def shard(step, parity, first=0, size=None):
        size = dsh if size is None else size
        return pl.ds(pl.multiple_of(shard_of(step, parity) * dsh + first, 16), size)

    theirs = pl.ds(hidden, hidden)
    down_copies = [
        push(SIB_DOWN, step, down_t.at[shard(step, 1 - core)], down_all.at[pl.ds(step * dsh, dsh), theirs], sib)
        for step in range(nx)
    ]
    loads[4].wait()
    down_t[...] = down_v[...].T
    for step in range(nx):
        down_copies[step].start()
        down_all[step * dsh:(step + 1) * dsh, 0:hidden] = down_t[shard(step, core), :]
    loads[3].wait()
    up_t[...] = up_v[...].T
    loads[2].wait()

    def gather_copy(kind, c):
        step, first, size, partner = {
            OWN_RA: (0, 0, cut, right),
            OWN_RB: (0, cut, dsh - cut, right),
            OWN_LA: (0, 0, cut, left),
            OWN_LB: (0, cut, dsh - cut, left),
            FWD_R: (nx - 1, 0, cut, right),
            FWD_L: (1, cut, dsh - cut, left),
            SIB_OWN: (0, 0, dsh, sib),
            SIB_L: (nx - 1, 0, dsh, sib),
            SIB_R: (1, 0, dsh, sib),
            SIB_FA: (2, 0, cut, sib),
            SIB_FB: (2, cut, dsh - cut, sib),
        }[kind]
        ref = feats.at[shard(step, core, first, size), lanes(gather_at[c])]
        return push(kind, c, ref, ref, partner)

    def hid_copy(c):
        at = lanes(hidden_at[c])
        return push(SIB_HID, c, hid.at[pl.ds(0, hidden), at], hid.at[theirs, at], sib)

    def sum_copy(kind, c):
        at = lanes(return_at[c])
        if kind == HALF_R:
            return push(kind, c, sums.at[2, pl.ds(0, cut), at], half_l.at[:, at], right)
        if kind == HALF_L:
            return push(kind, c, sums.at[2, pl.ds(cut, dsh - cut), at], half_r.at[:, at], left)
        place, ref, partner = (1, full_l, right) if kind in (SUM_RA, SUM_RB) else (0, full_r, left)
        rows = pl.ds(0, cut) if kind in (SUM_RA, SUM_LA) else pl.ds(cut, dsh - cut)
        return push(kind, c, sums.at[place, rows, at], ref.at[rows, at], partner)

    def arrive(c):
        start, size = gather_at[c]
        own = cap if start == 0 else 0
        ref = rows_in.at[pl.ds(start * unit + own, size * unit - own)]
        pltpu.make_async_copy(ref, ref, a2a_recv.at[c]).wait()
        turned = rows_in[start * unit:(start + size) * unit, :].T
        feats[shard(0, core), lanes(gather_at[c])] = turned[0:dsh, :]
        for kind in (OWN_RA, OWN_LB, OWN_RB, OWN_LA, SIB_OWN):
            gather_copy(kind, c).start()

    def forward(c):
        gather_copy(OWN_RA, c).wait_recv()
        gather_copy(FWD_R, c).start()
        gather_copy(OWN_LB, c).wait_recv()
        gather_copy(FWD_L, c).start()

    def to_sibling(c):
        gather_copy(OWN_RB, c).wait_recv()
        gather_copy(SIB_L, c).start()
        gather_copy(OWN_LA, c).wait_recv()
        gather_copy(SIB_R, c).start()
        gather_copy(FWD_R, c).wait_recv()
        gather_copy(SIB_FA, c).start()
        gather_copy(FWD_L, c).wait_recv()
        gather_copy(SIB_FB, c).start()

    gathered = set()

    def overlaps(piece, other):
        return piece[0] < other[0] + other[1] and other[0] < piece[0] + piece[1]

    def up(c):
        for i, piece in enumerate(gather_at):
            if overlaps(piece, hidden_at[c]) and i not in gathered:
                gathered.add(i)
                for kind in (SIB_OWN, SIB_L, SIB_R, SIB_FA, SIB_FB):
                    gather_copy(kind, i).wait_recv()
        at = lanes(hidden_at[c])
        hid[0:hidden, at] = gelu(jnp.dot(up_t[...], feats[:, at], preferred_element_type=F32)).astype(BF16)
        hid_copy(c).start()

    exchanged = set()

    def down(c):
        if not exchanged:
            for copy in down_copies:
                copy.wait_recv()
        for i, piece in enumerate(hidden_at):
            if overlaps(piece, return_at[c]) and i not in exchanged:
                exchanged.add(i)
                hid_copy(i).wait_recv()
        at = lanes(return_at[c])

        def term(step):
            return jnp.dot(down_all[step * dsh:(step + 1) * dsh, :], hid[:, at], preferred_element_type=F32)

        sums[2, :, at] = term(2).astype(BF16)
        sum_copy(HALF_R, c).start()
        sum_copy(HALF_L, c).start()
        one = term(1)
        sums[1, cut:dsh, at] = one[cut:dsh].astype(BF16)
        sum_copy(SUM_RB, c).start()
        acc[1, 0:cut, at] = one[0:cut]
        last = term(nx - 1)
        sums[0, 0:cut, at] = last[0:cut].astype(BF16)
        sum_copy(SUM_LA, c).start()
        acc[1, cut:dsh, at] = last[cut:dsh]
        acc[0, :, at] = term(0)

    def add_half(c):
        at = lanes(return_at[c])
        sum_copy(HALF_R, c).wait_recv()
        sums[1, 0:cut, at] = (acc[1, 0:cut, at] + half_l[:, at].astype(F32)).astype(BF16)
        sum_copy(SUM_RA, c).start()
        sum_copy(HALF_L, c).wait_recv()
        sums[0, cut:dsh, at] = (acc[1, cut:dsh, at] + half_r[:, at].astype(F32)).astype(BF16)
        sum_copy(SUM_LB, c).start()

    def finish(c):
        start, size = return_at[c]
        at = lanes(return_at[c])
        for kind in (SUM_RA, SUM_RB, SUM_LA, SUM_LB):
            sum_copy(kind, c).wait_recv()
        done = acc[0, :, at] + full_l[:, at].astype(F32) + full_r[:, at].astype(F32)
        if width > dsh:
            done = jnp.concatenate([done, jnp.zeros((width - dsh, size * unit), F32)], axis=0)
        back[start * unit:(start + size) * unit, :] = done.astype(BF16).T

        def give_back(k, carry):
            dy, dz = shift(k)
            to = ((y + ny - dy) % ny) * nz + (z + nz - dz) % nz
            pltpu.make_async_remote_copy(
                src_ref=back.at[block(k)], dst_ref=rows_out.at[block(e)],
                send_sem=back_send, recv_sem=back_recv,
                device_id={"expert": to}, device_id_type=MESH,
            ).start()
            return carry

        lax.fori_loop(max(1, start * ny), (start + size) * ny, give_back, 0)

    stages = dict(A=arrive, F=forward, L=to_sibling, U=up, D=down, H=add_half, E=finish)
    for op, c in order:
        stages[op](c)

    rows_out[block(e), :] = back[0:cap, :]
    for copy in down_copies:
        copy.wait_send()
    for c in range(len(gather_at)):
        for kind in range(SIB_HID):
            gather_copy(kind, c).wait_send()
    for c in range(len(hidden_at)):
        hid_copy(c).wait_send()
    for c in range(len(return_at)):
        for kind in (HALF_R, HALF_L, SUM_RA, SUM_RB, SUM_LA, SUM_LB):
            sum_copy(kind, c).wait_send()
    rest = pl.ds(0, slots - cap)
    pltpu.make_async_copy(send.at[rest], send.at[rest], a2a_send).wait()
    pltpu.make_async_copy(back.at[rest], back.at[rest], back_send).wait()
    pltpu.make_async_copy(rows_out.at[rest], rows_out.at[rest], back_recv).wait()

    turned = rows_out[...].T[0:dsh, :]
    total = jnp.zeros((dsh, count), F32)
    for k in range(TOP):
        total = total + gates_v[k:k + 1, :] * jnp.dot(turned, onehot[k], preferred_element_type=F32)
    out_ref[...] = total.astype(BF16)


def local(patches, expert_ids, gate_values, w_up, w_down):
    experts = lax.axis_size("expert")
    nt = lax.axis_size("tensor")
    count, dsh = patches.shape
    width = (dsh + 127) // 128 * 128
    model, hidden = w_up.shape[1:]
    cap = 21 * TOP * count // (20 * experts)
    slots = experts * cap
    ny = next(n for n in range(1, experts + 1) if n * n >= experts)
    nz = experts // ny
    nx = nt // 2
    cut = (dsh // 16 + 1) // 2 * 16
    gather, hiddens, returns, order = plan(nz)
    pieces = tuple(pieces_of(sizes) for sizes in (gather, hiddens, returns))
    most = max(nx, *(len(p) for p in pieces))
    hbm = pl.BlockSpec(memory_space=pl.ANY)
    dma = pltpu.SemaphoreType.DMA
    mixed = pl.pallas_call(
        functools.partial(layer_kernel, (ny, nz, nt, cap, dsh, hidden), pieces, order),
        out_shape=jax.ShapeDtypeStruct((dsh, count), BF16),
        in_specs=[hbm] * 5,
        out_specs=pl.BlockSpec(memory_space=pltpu.VMEM),
        scratch_shapes=[
            pltpu.VMEM((width, count), BF16),
            pltpu.VMEM((TOP, count), jnp.int32),
            pltpu.VMEM((TOP, count), F32),
            pltpu.VMEM((model, hidden), BF16),
            pltpu.VMEM((hidden, model), BF16),
            pltpu.VMEM((hidden, model), BF16),
            pltpu.VMEM((model, hidden), BF16),
            pltpu.VMEM((nx * dsh, 2 * hidden), BF16),
            pltpu.VMEM((TOP, slots, count), BF16),
            pltpu.VMEM((slots, width), BF16),
            pltpu.VMEM((slots, width), BF16),
            pltpu.VMEM((model, slots), BF16),
            pltpu.VMEM((2 * hidden, slots), BF16),
            pltpu.VMEM((2, dsh, slots), F32),
            pltpu.VMEM((3, dsh, slots), BF16),
            pltpu.VMEM((cut, slots), BF16),
            pltpu.VMEM((dsh - cut, slots), BF16),
            pltpu.VMEM((dsh, slots), BF16),
            pltpu.VMEM((dsh, slots), BF16),
            pltpu.VMEM((slots, width), BF16),
            pltpu.VMEM((slots, width), BF16),
            dma((5,)),
            dma,
            dma((len(gather),)),
            dma,
            dma,
            dma((KINDS, most)),
            dma((KINDS, most)),
        ],
        compiler_params=pltpu.CompilerParams(
            collective_id=0, has_side_effects=True, vmem_limit_bytes=VMEM_LIMIT
        ),
        cost_estimate=pl.CostEstimate(
            flops=4 * slots * model * hidden, bytes_accessed=4 * model * hidden, transcendentals=0
        ),
    )(patches.T, expert_ids.T, gate_values.T, w_up[0], w_down[0])
    return mixed.T


def solution(mesh):
    in_specs = (
        P("expert", "tensor"),
        P("expert", None),
        P("expert", None),
        P("expert", None, "tensor"),
        P("expert", "tensor", None),
    )
    out_specs = P("expert", "tensor")
    return jax.shard_map(local, mesh=mesh, in_specs=in_specs, out_specs=out_specs, check_vma=False)
```

time: 78.9 us -> 71.1 us (0.901)
  the two profiles are of different devices: /device:TPU:8 before, /device:TPU:1 now
where the time goes in v2:
time: 71.1 us; the launch traced here: 71 us
  Pallas kernels  69.4 us (98%)
  local copies, waits for them, and re-layouts  1.63 us (2%)
    pallas_call x1, Pallas kernels, local(): pl.pallas_call(functools.partial(layer_kernel, (ny, nz, nt, cap, dsh, hid...  69.4 us
    unnamed x1, local copies, waits for them, and re-layouts  1.63 us

profile of v2, /device:TPU:1, one launch (start us, length us, event | category | flops | bytes accessed | tf_op | source)
XLA Modules:
  0.0 71.0 jit_solution(13655426548930945139)
XLA Ops:
  0.0 69.4 %shard_map.55 = bf16[208,512]{1,0:T(8,128)(2,1)} custom-call(bf16[208,512]{1,0:T(8,128)(2,1)} %bitcast.9, s32[2,512]{1,0:T(2,128)} %bitcast.10, f32[2,512]{1,0:T(2,128)} %bitcast.11, bf16[1664,512]{1,0:T(8,128)(2,1)} %bitcast.7, bf16[512,1664]{1,0:T(8,128)(2,1)} %bitcast.8), custom_call_target="tpu_custom_call" | custom-call | flops 3489660928 | bytes 3407872 | tf_op jit(solution)/shard_map/pallas_call | solution.py:362
  69.4 1.6 %copy.7 = bf16[512,208]{0,1:T(8,128)(2,1)} copy(bf16[512,208]{0,1:T(8,128)(2,1)} %bitcast.6) | data formatting | bytes 425984

commit v3 on v2

--- a/solution.py
+++ b/solution.py
@@ -43,6 +43,21 @@
         return GATHER, HIDDEN, RETURN, ORDER
     ones = (1,) * groups
     return ones, ones, ones, tuple((op, at) for at in range(groups) for op in "AFLUDHE")
+
+
+def farthest_first(ny, nz):
+    def hops(step, size):
+        return min(step, size - step)
+
+    order = sorted((-hops(dy, ny) - hops(dz, nz), dy, dz) for dy in range(ny) for dz in range(nz))
+    return [(dy, dz) for _, dy, dz in order[:-1]]
+
+
+def shifts_of(ny, nz):
+    far = farthest_first(ny, nz)
+    parts = [far[at::4] for at in range(4)]
+    parts = sorted(parts, key=len)
+    return [(0, 0)] + [shift for part in parts for shift in part]
 
 
 def layer_kernel(
@@ -83,11 +98,9 @@
 
     barrier = pltpu.get_barrier_semaphore()
 
-    def greet(k, carry):
-        pl.semaphore_signal(barrier, inc=1, device_id={"expert": (e + k) % experts}, device_id_type=MESH)
-        return carry
-
-    lax.fori_loop(1, experts, greet, 0)
+    for dy, dz in farthest_first(ny, nz):
+        to = ((y + dy) % ny) * nz + (z + dz) % nz
+        pl.semaphore_signal(barrier, inc=1, device_id={"expert": to}, device_id_type=MESH)
     for partner in (right, left, sib):
         pl.semaphore_signal(barrier, inc=1, device_id={"tensor": partner}, device_id_type=MESH)
 
@@ -97,13 +110,10 @@
     def shard_of(step, parity):
         return ((x + step) % nx) * 2 + parity
 
-    def shift(k):
-        dy = k % ny
-        dz = (k // ny + ny * nz - dy) % nz
-        return dy, dz
+    shifts = shifts_of(ny, nz)
 
     def block(at):
-        return pl.ds(pl.multiple_of(at * cap, cap), cap)
+        return pl.ds(at * cap if isinstance(at, int) else pl.multiple_of(at * cap, cap), cap)
 
     def lanes(piece):
         start, size = piece
@@ -147,17 +157,14 @@
     pl.semaphore_wait(barrier, experts - 1 + 3)
 
     for index, (start, size) in enumerate(gather_at):
-        def send_out(k, carry, index=index):
-            dy, dz = shift(k)
+        for k in range(max(1, start * ny), (start + size) * ny):
+            dy, dz = shifts[k]
             to = ((y + dy) % ny) * nz + (z + dz) % nz
             pltpu.make_async_remote_copy(
                 src_ref=send.at[block(to)], dst_ref=rows_in.at[block(k)],
                 send_sem=a2a_send, recv_sem=a2a_recv.at[index],
                 device_id={"expert": to}, device_id_type=MESH,
             ).start()
-            return carry
-
-        lax.fori_loop(max(1, start * ny), (start + size) * ny, send_out, 0)
     rows_in[0:cap, :] = send[block(e), :]
 
     def push(kind, c, src, dst, partner):
@@ -303,17 +310,14 @@
             done = jnp.concatenate([done, jnp.zeros((width - dsh, size * unit), F32)], axis=0)
         back[start * unit:(start + size) * unit, :] = done.astype(BF16).T
 
-        def give_back(k, carry):
-            dy, dz = shift(k)
+        for k in range(max(1, start * ny), (start + size) * ny):
+            dy, dz = shifts[k]
             to = ((y + ny - dy) % ny) * nz + (z + nz - dz) % nz
             pltpu.make_async_remote_copy(
                 src_ref=back.at[block(k)], dst_ref=rows_out.at[block(e)],
                 send_sem=back_send, recv_sem=back_recv,
                 device_id={"expert": to}, device_id_type=MESH,
             ).start()
-            return carry
-
-        lax.fori_loop(max(1, start * ny), (start + size) * ny, give_back, 0)
 
     stages = dict(A=arrive, F=forward, L=to_sibling, U=up, D=down, H=add_half, E=finish)
     for op, c in order:

time: 71.1 us -> 69.1 us (0.972)
  Pallas kernels: 69.4 us -> 67.3 us
    pallas_call x1, Pallas kernels: 69.4 us -> 67.3 us  [local(): pl.pallas_call(functools.partial(layer_kernel, (ny, nz, nt, cap, dsh, hid...]
where the time goes in v3:
time: 69.1 us; the launch traced here: 68.9 us
  Pallas kernels  67.3 us (97%)
  local copies, waits for them, and re-layouts  1.63 us (2%)
    pallas_call x1, Pallas kernels, local(): pl.pallas_call(functools.partial(layer_kernel, (ny, nz, nt, cap, dsh, hid...  67.3 us
    unnamed x1, local copies, waits for them, and re-layouts  1.63 us

profile of v3, /device:TPU:1, one launch (start us, length us, event | category | flops | bytes accessed | tf_op | source)
XLA Modules:
  0.0 68.9 jit_solution(6035690142132947219)
XLA Ops:
  0.0 67.3 %shard_map.55 = bf16[208,512]{1,0:T(8,128)(2,1)} custom-call(bf16[208,512]{1,0:T(8,128)(2,1)} %bitcast.9, s32[2,512]{1,0:T(2,128)} %bitcast.10, f32[2,512]{1,0:T(2,128)} %bitcast.11, bf16[1664,512]{1,0:T(8,128)(2,1)} %bitcast.7, bf16[512,1664]{1,0:T(8,128)(2,1)} %bitcast.8), custom_call_target="tpu_custom_call" | custom-call | flops 3489660928 | bytes 3407872 | tf_op jit(solution)/shard_map/pallas_call | solution.py:366
  67.3 1.6 %copy.7 = bf16[512,208]{0,1:T(8,128)(2,1)} copy(bf16[512,208]{0,1:T(8,128)(2,1)} %bitcast.6) | data formatting | bytes 425984

commit v4 on v3

--- a/solution.py
+++ b/solution.py
@@ -112,8 +112,12 @@
 
     shifts = shifts_of(ny, nz)
 
-    def block(at):
-        return pl.ds(at * cap if isinstance(at, int) else pl.multiple_of(at * cap, cap), cap)
+    def away(k):
+        dy, dz = shifts[k]
+        return ((y + dy) % ny) * nz + (z + dz) % nz
+
+    def block(k):
+        return pl.ds(k * cap, cap)
 
     def lanes(piece):
         start, size = piece
@@ -139,33 +143,29 @@
 
     tile = min(256, slots)
 
-    def place(i, carry):
-        at = pl.ds(pl.multiple_of(i * tile, tile), tile)
-        slot = (lax.broadcasted_iota(jnp.int32, (tile, count), 0) + i * tile).astype(F32)
+    offset = lax.broadcasted_iota(jnp.int32, (cap, count), 0)
+    for start in range(0, slots, tile):
+        held = range(start // cap, (start + tile) // cap)
+        slot = jnp.concatenate([away(k) * cap + offset for k in held], axis=0).astype(F32)
         both = jnp.zeros((tile, count), F32)
         for k in range(TOP):
             hit = (slot == targets[k]).astype(F32)
-            onehot[k, at, :] = hit.astype(BF16)
+            onehot[k, start:start + tile, :] = hit.astype(BF16)
             both = both + hit
-        send[at, :] = lax.dot_general(
+        send[start:start + tile, :] = lax.dot_general(
             both.astype(BF16), patches_v[...], (((1,), (1,)), ((), ())), preferred_element_type=F32
         ).astype(BF16)
-        return carry
-
-    lax.fori_loop(0, slots // tile, place, 0)
 
     pl.semaphore_wait(barrier, experts - 1 + 3)
 
     for index, (start, size) in enumerate(gather_at):
         for k in range(max(1, start * ny), (start + size) * ny):
-            dy, dz = shifts[k]
-            to = ((y + dy) % ny) * nz + (z + dz) % nz
             pltpu.make_async_remote_copy(
-                src_ref=send.at[block(to)], dst_ref=rows_in.at[block(k)],
+                src_ref=send.at[block(k)], dst_ref=rows_in.at[block(k)],
                 send_sem=a2a_send, recv_sem=a2a_recv.at[index],
-                device_id={"expert": to}, device_id_type=MESH,
+                device_id={"expert": away(k)}, device_id_type=MESH,
             ).start()
-    rows_in[0:cap, :] = send[block(e), :]
+    rows_in[0:cap, :] = send[0:cap, :]
 
     def push(kind, c, src, dst, partner):
         return pltpu.make_async_remote_copy(
@@ -314,8 +314,8 @@
             dy, dz = shifts[k]
             to = ((y + ny - dy) % ny) * nz + (z + nz - dz) % nz
             pltpu.make_async_remote_copy(
-                src_ref=back.at[block(k)], dst_ref=rows_out.at[block(e)],
-                send_sem=back_send, recv_sem=back_recv,
+                src_ref=back.at[block(k)], dst_ref=rows_out.at[block(k)],
+                send_sem=back_send, recv_sem=back_recv.at[c],
                 device_id={"expert": to}, device_id_type=MESH,
             ).start()
 
@@ -323,7 +323,7 @@
     for op, c in order:
         stages[op](c)
 
-    rows_out[block(e), :] = back[0:cap, :]
+    rows_out[0:cap, :] = back[0:cap, :]
     for copy in down_copies:
         copy.wait_send()
     for c in range(len(gather_at)):
@@ -337,12 +337,16 @@
     rest = pl.ds(0, slots - cap)
     pltpu.make_async_copy(send.at[rest], send.at[rest], a2a_send).wait()
     pltpu.make_async_copy(back.at[rest], back.at[rest], back_send).wait()
-    pltpu.make_async_copy(rows_out.at[rest], rows_out.at[rest], back_recv).wait()
-
-    turned = rows_out[...].T[0:dsh, :]
+
     total = jnp.zeros((dsh, count), F32)
-    for k in range(TOP):
-        total = total + gates_v[k:k + 1, :] * jnp.dot(turned, onehot[k], preferred_element_type=F32)
+    for c, (start, size) in enumerate(return_at):
+        own = cap if start == 0 else 0
+        ref = rows_out.at[pl.ds(start * unit + own, size * unit - own)]
+        pltpu.make_async_copy(ref, ref, back_recv.at[c]).wait()
+        rows = slice(start * unit, (start + size) * unit)
+        turned = rows_out[rows, :].T[0:dsh, :]
+        for k in range(TOP):
+            total = total + gates_v[k:k + 1, :] * jnp.dot(turned, onehot[k, rows, :], preferred_element_type=F32)
     out_ref[...] = total.astype(BF16)
 
 
@@ -394,7 +398,7 @@
             dma,
             dma((len(gather),)),
             dma,
-            dma,
+            dma((len(returns),)),
             dma((KINDS, most)),
             dma((KINDS, most)),
         ],

time: 69.1 us -> 68.4 us (0.990)
  Pallas kernels: 67.3 us -> 66.5 us
    pallas_call x1, Pallas kernels: 67.3 us -> 66.5 us  [local(): pl.pallas_call(functools.partial(layer_kernel, (ny, nz, nt, cap, dsh, hid...]
where the time goes in v4:
time: 68.4 us; the launch traced here: 68.1 us
  Pallas kernels  66.5 us (97%)
  local copies, waits for them, and re-layouts  1.63 us (2%)
    pallas_call x1, Pallas kernels, local(): pl.pallas_call(functools.partial(layer_kernel, (ny, nz, nt, cap, dsh, hid...  66.5 us
    unnamed x1, local copies, waits for them, and re-layouts  1.63 us

profile of v4, /device:TPU:1, one launch (start us, length us, event | category | flops | bytes accessed | tf_op | source)
XLA Modules:
  0.0 68.1 jit_solution(13552613382712577504)
XLA Ops:
  0.0 66.5 %shard_map.55 = bf16[208,512]{1,0:T(8,128)(2,1)} custom-call(bf16[208,512]{1,0:T(8,128)(2,1)} %bitcast.9, s32[2,512]{1,0:T(2,128)} %bitcast.10, f32[2,512]{1,0:T(2,128)} %bitcast.11, bf16[1664,512]{1,0:T(8,128)(2,1)} %bitcast.7, bf16[512,1664]{1,0:T(8,128)(2,1)} %bitcast.8), custom_call_target="tpu_custom_call" | custom-call | flops 3489660928 | bytes 3407872 | tf_op jit(solution)/shard_map/pallas_call | solution.py:370
  66.5 1.6 %copy.7 = bf16[512,208]{0,1:T(8,128)(2,1)} copy(bf16[512,208]{0,1:T(8,128)(2,1)} %bitcast.6) | data formatting | bytes 425984

commit v5 on v4

--- a/solution.py
+++ b/solution.py
@@ -21,11 +21,11 @@
 HIDDEN = (2, 2, 2, 2)
 RETURN = (2, 2, 2, 2)
 ORDER = (
-    ("A", 0), ("A", 1), ("F", 0), ("F", 1), ("A", 2), ("L", 0),
-    ("A", 3), ("L", 1), ("U", 0), ("F", 2), ("U", 1), ("F", 3),
-    ("D", 0), ("L", 2), ("D", 1), ("U", 2), ("L", 3), ("H", 0),
-    ("D", 2), ("H", 1), ("U", 3), ("E", 0), ("H", 2), ("D", 3),
-    ("E", 1), ("E", 2), ("H", 3), ("E", 3),
+    ("A", 0), ("A", 1), ("F", 0), ("A", 2), ("F", 1), ("L", 0),
+    ("A", 3), ("U", 0), ("F", 2), ("L", 1), ("U", 1), ("F", 3),
+    ("D", 0), ("L", 2), ("D", 1), ("L", 3), ("U", 2), ("H", 0),
+    ("D", 2), ("U", 3), ("H", 1), ("E", 0), ("D", 3), ("H", 2),
+    ("E", 1), ("H", 3), ("E", 2), ("E", 3),
 )
 
 

time: 68.4 us -> 69.9 us (1.022)
  Pallas kernels: 66.5 us -> 67.8 us
    pallas_call x1, Pallas kernels: 66.5 us -> 67.8 us  [local(): pl.pallas_call(functools.partial(layer_kernel, (ny, nz, nt, cap, dsh, hid...]
where the time goes in v5:
time: 69.9 us; the launch traced here: 69.4 us
  Pallas kernels  67.8 us (97%)
  local copies, waits for them, and re-layouts  1.63 us (2%)
    pallas_call x1, Pallas kernels, local(): pl.pallas_call(functools.partial(layer_kernel, (ny, nz, nt, cap, dsh, hid...  67.8 us
    unnamed x1, local copies, waits for them, and re-layouts  1.63 us

profile of v5, /device:TPU:1, one launch (start us, length us, event | category | flops | bytes accessed | tf_op | source)
XLA Modules:
  0.0 69.4 jit_solution(9290221435346679902)
XLA Ops:
  0.0 67.8 %shard_map.55 = bf16[208,512]{1,0:T(8,128)(2,1)} custom-call(bf16[208,512]{1,0:T(8,128)(2,1)} %bitcast.9, s32[2,512]{1,0:T(2,128)} %bitcast.10, f32[2,512]{1,0:T(2,128)} %bitcast.11, bf16[1664,512]{1,0:T(8,128)(2,1)} %bitcast.7, bf16[512,1664]{1,0:T(8,128)(2,1)} %bitcast.8), custom_call_target="tpu_custom_call" | custom-call | flops 3489660928 | bytes 3407872 | tf_op jit(solution)/shard_map/pallas_call | solution.py:370
  67.8 1.6 %copy.7 = bf16[512,208]{0,1:T(8,128)(2,1)} copy(bf16[512,208]{0,1:T(8,128)(2,1)} %bitcast.6) | data formatting | bytes 425984
